TPU v7x, 32 devices: a whole 2x2x4 slice. The times are simulated.
32 devices in a mesh: dev: 32 (over z, y, x, core).
Axes of the slice: x: 2, y: 2, z: 4, core: 2. Of those that a mesh axis runs over, the one named last changes fastest.
Arguments:
- source_rows: bfloat16 [32768, 4096], P('dev'), may hold values from -6 to 6
- factor: bfloat16 [8, 512, 512], replicated, may hold values from -0.25 to 0.25
- plan_start: int32 [32, 32], replicated, may hold values from 0 to 992, as said below
- plan_count: int32 [32, 32], replicated, may hold values from 0 to 32, as said below
- partners: int32 [2, 32], replicated, may hold values from 0 to 31, as said below
Outputs:
- kernel_tiles: float32 [2, 16384, 512], P(None, 'dev')
Inputs may be any that keep to these rules, and one draw needn't show every extreme that they name: `plan_count`: entry [s, d] is how many rows source shard s sends to destination d; each column sums to exactly 512; one source's counts sum to at most 1024, and some source reaches it. `plan_start`: the row ranges of one source for the different destinations are disjoint and lie within its 1024 rows. In each round r there is one power of two m_r with partners[r, d] = d XOR m_r for every player d; the m_r of different rounds differ.
All inputs are finite; a program needn't handle non-finite values.
Results may differ from a plain program's by a relative error of at most 0.0029.
Values may be sent and summed in bfloat16 or wider, within the bound.
A program may use at most 128 MiB of HBM per device.

v0:
```python
from functools import partial

import jax
import jax.numpy as jnp
from jax import lax
from jax.experimental import pallas as pl
from jax.experimental.pallas import tpu as pltpu
from jax.sharding import PartitionSpec as P

VMEM_BYTES = 56 * 1024 * 1024


def scatter_kernel(
    dest_ref, place_ref, picked_ref, rows_ref, factor_ref, out_ref, select, stage, sem
):
    layer = pl.program_id(0)
    layers = pl.num_programs(0)
    players, slot_rows, width = stage.shape[1:]
    capacity = rows_ref.shape[0]
    per_part = layers // 4
    part = layer // per_part
    buf = lax.rem(layer, 2)

    @pl.when(layer == 0)
    def _():
        lanes = lax.broadcasted_iota(jnp.int32, select.shape, 1)
        select[...] = (lanes == picked_ref[...]).astype(jnp.float32).astype(jnp.bfloat16)

    conditioned = jnp.dot(
        rows_ref[...], factor_ref[0], preferred_element_type=jnp.float32
    ).astype(jnp.bfloat16)

    def drain(which):
        pltpu.make_async_copy(stage.at[which], stage.at[which], sem.at[which]).wait()

    @pl.when(layer >= 2)
    def _():
        drain(buf)

    moved = jnp.dot(select[...], conditioned, preferred_element_type=jnp.float32)
    stage[buf] = moved.reshape(players, slot_rows, width).astype(jnp.bfloat16)
    column = pl.multiple_of(lax.rem(layer, per_part) * width, width)

    @pl.loop(0, players)
    def _(player):
        at = part * players + player
        pltpu.make_async_copy(
            stage.at[buf, player],
            out_ref.at[dest_ref[at], place_ref[at], :, pl.ds(column, width)],
            sem.at[buf],
        ).start()

    @pl.when(layer == layers - 1)
    def _():
        drain(1 - buf)
        drain(buf)


def tiles_kernel(mate_ref, arrival_ref, received_ref, own_ref, s1_ref, s2_ref, s3_ref, blocks, *, scaling):
    step = pl.program_id(0)
    sources, _, slot_rows, width = received_ref.shape
    rows = arrival_ref.shape[1]
    lanes = lax.broadcasted_iota(jnp.int32, (rows, sources * slot_rows), 1)
    select = (lanes == arrival_ref[0]).astype(jnp.float32).astype(jnp.bfloat16)
    data = received_ref[:, 0]
    if slot_rows % 16:
        data = data.astype(jnp.float32).reshape(sources * slot_rows, width).astype(jnp.bfloat16)
    else:
        data = data.reshape(sources * slot_rows, width)
    blocks[step] = jnp.dot(select, data, preferred_element_type=jnp.float32).astype(jnp.bfloat16)

    def tile(a, b):
        return lax.dot_general(
            blocks[a], blocks[b], (((1,), (1,)), ((), ())), preferred_element_type=jnp.float32
        )

    @pl.when(step == 3)
    def _():
        for r in range(2):
            mate = mate_ref[r]
            own_ref[r] = tile(0, mate) * scaling
            for j, ref in ((1, s1_ref), (2, s2_ref), (3, s3_ref)):
                ref[r] = (tile(j, j ^ mate) * scaling).astype(jnp.bfloat16)


def exchange(low, high, own, s1, s2, s3):
    devices = lax.axis_size("dev")
    total = own
    for value, mask in ((s3, low ^ high), (s1, low), (s2, high)):
        got = lax.ppermute(value, "dev", [(d, d ^ mask) for d in range(devices)])
        total = total + got.astype(jnp.float32)
    return total


def per_device(source_rows, factor, plan_start, plan_count, partners):
    devices = lax.axis_size("dev")
    own_index = lax.axis_index("dev")
    capacity, feat_width = source_rows.shape
    layers, width, _ = factor.shape
    slot_rows = capacity // devices
    block_rows = capacity // 2
    part_width = feat_width // 4
    i32 = jnp.int32

    low = jnp.minimum(partners[0, 0], partners[1, 0])
    high = jnp.maximum(partners[0, 0], partners[1, 0])
    mates = jnp.where(partners[:, 0] == low, 1, 2).astype(i32)

    player = jnp.arange(devices, dtype=i32)[None, :]
    part = jnp.arange(4, dtype=i32)[:, None]
    dest = (player & ~low & ~high) | jnp.where(part & 1, low, 0) | jnp.where(part & 2, high, 0)
    differs = player ^ dest
    place = jnp.where(differs & low, 1, 0) + jnp.where(differs & high, 2, 0)
    dest, place = dest.reshape(-1).astype(i32), place.reshape(-1).astype(i32)

    start_row = lax.dynamic_index_in_dim(plan_start, own_index, 0, keepdims=False)
    count_row = lax.dynamic_index_in_dim(plan_count, own_index, 0, keepdims=False)
    offsets = jnp.arange(slot_rows, dtype=i32)
    usable = offsets[None, :] < count_row[:, None]
    picked = jnp.where(usable, start_row[:, None] + offsets[None, :], -1).reshape(-1, 1)

    send = pl.pallas_call(
        scatter_kernel,
        out_shape=jax.ShapeDtypeStruct((devices, 4, slot_rows, part_width), jnp.bfloat16),
        grid_spec=pltpu.PrefetchScalarGridSpec(
            num_scalar_prefetch=2,
            grid=(layers,),
            in_specs=[
                pl.BlockSpec((capacity, 1), lambda l, *_: (0, 0)),
                pl.BlockSpec((capacity, width), lambda l, *_: (0, l)),
                pl.BlockSpec((1, width, width), lambda l, *_: (l, 0, 0)),
            ],
            out_specs=pl.BlockSpec(memory_space=pl.ANY),
            scratch_shapes=[
                pltpu.VMEM((capacity, capacity), jnp.bfloat16),
                pltpu.VMEM((2, devices, slot_rows, width), jnp.bfloat16),
                pltpu.SemaphoreType.DMA((2,)),
            ],
        ),
        compiler_params=pltpu.CompilerParams(vmem_limit_bytes=VMEM_BYTES),
        name="condition_and_place",
    )(dest, place, picked, source_rows, factor)

    received = lax.all_to_all(send, "dev", split_axis=0, concat_axis=0, tiled=True)

    combos = jnp.stack([jnp.zeros_like(low), low, high, low | high])
    counts = jnp.take(plan_count, own_index ^ combos, axis=1).T
    inclusive = jnp.cumsum(counts, axis=1)
    exclusive = inclusive - counts
    positions = jnp.arange(block_rows, dtype=i32)
    source_of = jnp.sum((inclusive[:, None, :] <= positions[None, :, None]).astype(i32), axis=2)
    source_of = jnp.minimum(source_of, devices - 1)
    one_hot = (source_of[:, :, None] == jnp.arange(devices, dtype=i32)[None, None, :]).astype(i32)
    before = jnp.sum(one_hot * exclusive[:, None, :], axis=2)
    arrival = (source_of * slot_rows + positions[None, :] - before)[:, :, None]

    tile_shape = (2, block_rows, block_rows)
    whole_tile = pl.BlockSpec(tile_shape, lambda j, *_: (0, 0, 0))
    own, s1, s2, s3 = pl.pallas_call(
        partial(tiles_kernel, scaling=feat_width ** (-0.5)),
        out_shape=[jax.ShapeDtypeStruct(tile_shape, jnp.float32)]
        + [jax.ShapeDtypeStruct(tile_shape, jnp.bfloat16)] * 3,
        grid_spec=pltpu.PrefetchScalarGridSpec(
            num_scalar_prefetch=1,
            grid=(4,),
            in_specs=[
                pl.BlockSpec((1, block_rows, 1), lambda j, *_: (j, 0, 0)),
                pl.BlockSpec((devices, 1, slot_rows, part_width), lambda j, *_: (0, j, 0, 0)),
            ],
            out_specs=[whole_tile] * 4,
            scratch_shapes=[pltpu.VMEM((4, block_rows, part_width), jnp.bfloat16)],
        ),
        compiler_params=pltpu.CompilerParams(vmem_limit_bytes=VMEM_BYTES),
        name="compact_and_tiles",
    )(mates, arrival, received)

    levels = devices.bit_length() - 1
    branches, keys = [], []
    for b in range(levels):
        for a in range(b):
            branches.append(partial(exchange, 1 << a, 1 << b))
            keys.append((1 << a) | (1 << b))
    which = jnp.argmax(jnp.asarray(keys, dtype=i32) == (low | high)).astype(i32)
    return lax.switch(which, branches, own, s1, s2, s3)


def solution(mesh):
    placed = (P("dev", None), P(), P(), P(), P())
    return jax.shard_map(
        per_device, mesh=mesh, in_specs=placed, out_specs=P(None, "dev", None), check_vma=False
    )
```

profile of v0, /device:TPU:0, one launch (start us, length us, event | category | flops | bytes accessed | tf_op | source)
XLA Modules:
  0.0 284.1 jit_solution(6986932804802940604)
XLA Ops:
  0.0 1.3 fusion.3
  3.7 0.1 or_or_fusion
  3.8 0.1 or.42.dest_ref
  3.9 0.1 xor.35
  4.0 0.7 dynamic-slice_bitcast_fusion
  4.7 0.1 add_select_fusion
  4.7 1.3 select_n.93.picked_ref
  6.1 0.5 fusion.2.place_ref
  6.6 21.5 %condition_and_place.1 = bf16[32,4,32,1024]{3,2,1,0:T(8,128)(2,1)} custom-call(s32[128]{0:T(128)} %copy-done.2, s32[128]{0:T(128)} %fusion.2.place_ref, s32[1024,1]{1,0:T(8,128)} %select_n.93.picked_ref, bf16[1024,4096]{1,0:T(8,128)(2,1)} %rows_ref.1, bf16[8,512,512]{2,1,0:T(8,128)(2,1)} %factor_ref.1), custom_call_target="tpu_custom_call" | custom-call | tf_op jit(solution)/shard_map/condition_and_place/pallas_call | solution.py:122
  28.1 7.4 %all-to-all-start = ((bf16[32,4,32,1024]{3,2,1,0:T(8,128)(2,1)}), bf16[32,4,32,1024]{3,2,1,0:T(8,128)(2,1)}, u32[]{:S(2)}, u32[]{:S(2)}) async-start(bf16[32,4,32,1024]{3,2,1,0:T(8,128)(2,1)} %condition_and_place.1), calls=%async_computation | async-start | bytes 16777216 | tf_op jit(solution)/shard_map/all_to_all | solution.py:144
  35.6 0.1 fusion
  35.8 0.6 gather_fusion
  36.3 0.1 compare_and_fusion
  36.4 0.1 broadcast_select_fusion
  36.5 0.2 reduce_window_sum.11
  36.7 0.1 convert_reduce_fusion
  36.8 0.1 fusion.4
  36.9 0.1 select_reduce_fusion
  37.0 0.4 copy.28
  37.4 0.4 copy.27
  37.8 1.1 sub.14.arrival_ref
  38.9 0.7 compare_reduce_fusion
  40.3 0.6 fusion.1.mate_ref
  40.9 180.6 %all-to-all-done.received_ref = bf16[32,4,32,1024]{3,2,1,0:T(8,128)(2,1)} async-done(((bf16[32,4,32,1024]{3,2,1,0:T(8,128)(2,1)}), bf16[32,4,32,1024]{3,2,1,0:T(8,128)(2,1)}, u32[]{:S(2)}, u32[]{:S(2)}) %all-to-all-start) | async-done | bytes 8388640 | tf_op jit(solution)/shard_map/all_to_all | solution.py:144
  221.6 12.6 %compact_and_tiles.1 = (f32[2,512,512]{2,1,0:T(8,128)S(1)}, bf16[2,512,512]{2,1,0:T(8,128)(2,1)S(1)}, bf16[2,512,512]{2,1,0:T(8,128)(2,1)S(1)}, bf16[2,512,512]{2,1,0:T(8,128)(2,1)S(1)}) custom-call(s32[2]{0:T(128)} %fusion.1.mate_ref, s32[4,512,1]{2,1,0:T(8,128)} %sub.14.arrival_ref, bf16[32,4,32,1024]{3,2,1,0:T(8,128)(2,1)} %all-to-all-done.received_ref), custom_call_target="tpu_custom_call" | custom-call | tf_op jit(solution)/shard_map/compact_and_tiles/pallas_call | solution.py:159
  234.2 48.6 %conditional.1 = (f32[2,512,512]{2,1,0:T(8,128)S(1)}) conditional(s32[]{:T(128)} %clamp.3, (bf16[2,512,512]{2,1,0:T(8,128)(2,1)S(1)}, f32[2,512,512]{2,1,0:T(8,128)S(1)}, bf16[2,512,512]{2,1,0:T(8,128)(2,1)S(1)}, bf16[2,512,512]{2,1,0:T(8,128)(2,1)S(1)}) %tuple.37, (bf16[2,512,512]{2,1,0:T(8,128)(2,1)S(1)}, ...), branch_computations={%region_4.5_spmd, %region_5.6_spmd, %region_6.7_spmd, %region_7.8_... | conditional | flops 3145728 | bytes 19923072 | solution.py:184
  234.4 1.8 collective-permute-start.9
  236.2 0.8 collective-permute-done.10
  236.9 23.4 %collective-permute-done.11 = bf16[2,512,512]{2,1,0:T(8,128)(2,1)S(1)} collective-permute-done((bf16[2,512,512]{2,1,0:T(8,128)(2,1)S(1)}, bf16[2,512,512]{2,1,0:T(8,128)(2,1)S(1)}, u32[]{:S(2)}, u32[]{:S(2)}) %collective-permute-start.11) | collective-permute-done | bytes 1048608 | tf_op jit(solution)/shard_map/cond/branch_3_fun/ppermute | solution.py:90
  260.3 21.6 %collective-permute-done.9 = bf16[2,512,512]{2,1,0:T(8,128)(2,1)S(1)} collective-permute-done((bf16[2,512,512]{2,1,0:T(8,128)(2,1)S(1)}, bf16[2,512,512]{2,1,0:T(8,128)(2,1)S(1)}, u32[]{:S(2)}, u32[]{:S(2)}) %collective-permute-start.9) | collective-permute-done | bytes 1048608 | tf_op jit(solution)/shard_map/cond/branch_3_fun/ppermute | solution.py:90
  281.9 0.7 convert_add_fusion.3
  282.8 1.3 copy-done
  (18 shorter events, 0.3 us)
Async XLA Ops:
  3.9 2.7 copy-start.2
  28.1 7.5 %copy-start.1 = (s32[32,32]{1,0:T(8,128)S(1)}, s32[32,32]{1,0:T(8,128)}, u32[]{:S(2)}) copy-start(s32[32,32]{1,0:T(8,128)} %param.19) | copy-start | bytes 12292
  28.1 193.5 %all-to-all-start = ((bf16[32,4,32,1024]{3,2,1,0:T(8,128)(2,1)}), bf16[32,4,32,1024]{3,2,1,0:T(8,128)(2,1)}, u32[]{:S(2)}, u32[]{:S(2)}) async-start(bf16[32,4,32,1024]{3,2,1,0:T(8,128)(2,1)} %condition_and_place.1), calls=%async_computation | async-start | bytes 16777216 | tf_op jit(solution)/shard_map/all_to_all | solution.py:144
  37.4 1.5 copy-start.4
  37.4 2.9 %copy-start.3 = (s32[2,32]{1,0:T(2,128)S(1)}, s32[2,32]{1,0:T(2,128)}, u32[]{:S(2)}) copy-start(s32[2,32]{1,0:T(2,128)} %param.20) | copy-start | bytes 772
  234.2 2.7 collective-permute-start.10
  234.3 26.0 %collective-permute-start.11 = (bf16[2,512,512]{2,1,0:T(8,128)(2,1)S(1)}, bf16[2,512,512]{2,1,0:T(8,128)(2,1)S(1)}, u32[]{:S(2)}, u32[]{:S(2)}) collective-permute-start(bf16[2,512,512]{2,1,0:T(8,128)(2,1)S(1)} %get-tuple-element.111), channel_id=1, source_target_pairs={{0,8},{1,9},{2,10},{3,11},{4,12},{5,13},{6,14},{7,15},{8,0},{9,1},... | collective-permute-start | bytes 3145736 | tf_op jit(solution)/shard_map/cond/branch_3_fun/ppermute | solution.py:90
  234.4 47.5 %collective-permute-start.9 = (bf16[2,512,512]{2,1,0:T(8,128)(2,1)S(1)}, bf16[2,512,512]{2,1,0:T(8,128)(2,1)S(1)}, u32[]{:S(2)}, u32[]{:S(2)}) collective-permute-start(bf16[2,512,512]{2,1,0:T(8,128)(2,1)S(1)} %get-tuple-element.109), channel_id=1, source_target_pairs={{0,9},{1,8},{2,11},{3,10},{4,13},{5,12},{6,15},{7,14},{8,1},{9,0},... | collective-permute-start | bytes 3145736 | tf_op jit(solution)/shard_map/cond/branch_3_fun/ppermute | solution.py:90
  282.8 1.3 copy-start
where the time goes:
time: 284 us
  waiting for transfers between devices  226 us (80%)
  Pallas kernels  34.1 us (12%)
  starting transfers between devices  9.36 us (3%)
  local copies, waits for them, and re-layouts  6.2 us (2%)
  other arithmetic  4.57 us (2%)
  between operations  3.24 us (1%)
    all_to_all x1, waiting for transfers between devices, per_device(): lax.all_to_all(send, 'dev', split_axis=0, concat_axis=0, tiled=True)  181 us
    ppermute x3, waiting for transfers between devices, exchange(): got = lax.ppermute(value, 'dev', [(d, d ^ mask) for d in range(devices)])  45.7 us
    pallas_call x1, Pallas kernels, per_device(): pl.pallas_call(scatter_kernel, out_shape=jax.ShapeDtypeStruct((devices, 4...  21.5 us
    pallas_call x1, Pallas kernels, per_device(): pl.pallas_call(partial(tiles_kernel, scaling=feat_width ** (-0.5)), out_s...  12.6 us
    all_to_all x1, starting transfers between devices, per_device(): lax.all_to_all(send, 'dev', split_axis=0, concat_axis=0, tiled=True)  7.43 us
  transfers between devices with their start and end apart: 4, of which 4 were waited for; matrix products, arithmetic and copies ran while one was open for 2% of the time, Pallas kernels for 0%

commit v1 on v0

--- a/solution.py
+++ b/solution.py
@@ -56,7 +56,7 @@
         drain(buf)
 
 
-def tiles_kernel(mate_ref, arrival_ref, received_ref, own_ref, s1_ref, s2_ref, s3_ref, blocks, *, scaling):
+def tiles_kernel(edge_ref, arrival_ref, received_ref, own_ref, s1_ref, s2_ref, s3_ref, blocks, *, scaling):
     step = pl.program_id(0)
     sources, _, slot_rows, width = received_ref.shape
     rows = arrival_ref.shape[1]
@@ -76,11 +76,15 @@
 
     @pl.when(step == 3)
     def _():
-        for r in range(2):
-            mate = mate_ref[r]
-            own_ref[r] = tile(0, mate) * scaling
-            for j, ref in ((1, s1_ref), (2, s2_ref), (3, s3_ref)):
-                ref[r] = (tile(j, j ^ mate) * scaling).astype(jnp.bfloat16)
+        edge = edge_ref[0]
+        own_ref[...] = tile(0, edge) * scaling
+        s1_ref[...] = (tile(1, 1 ^ (3 - edge)) * scaling).astype(jnp.bfloat16)
+        s2_ref[...] = (tile(2, 2 ^ (3 - edge)) * scaling).astype(jnp.bfloat16)
+        s3_ref[...] = (tile(3, 3 ^ edge) * scaling).astype(jnp.bfloat16)
+
+
+def owned_mask(device, low, high):
+    return low if bool(device & low) == bool(device & high) else high
 
 
 def exchange(low, high, own, s1, s2, s3):
@@ -89,7 +93,12 @@
     for value, mask in ((s3, low ^ high), (s1, low), (s2, high)):
         got = lax.ppermute(value, "dev", [(d, d ^ mask) for d in range(devices)])
         total = total + got.astype(jnp.float32)
-    return total
+    other = lax.ppermute(
+        total.astype(jnp.bfloat16),
+        "dev",
+        [(d, d ^ owned_mask(d, low, high)) for d in range(devices)],
+    )
+    return total, other
 
 
 def per_device(source_rows, factor, plan_start, plan_count, partners):
@@ -105,6 +114,7 @@
     low = jnp.minimum(partners[0, 0], partners[1, 0])
     high = jnp.maximum(partners[0, 0], partners[1, 0])
     mates = jnp.where(partners[:, 0] == low, 1, 2).astype(i32)
+    edge = jnp.where(((own_index & low) != 0) == ((own_index & high) != 0), 1, 2).astype(i32)
 
     player = jnp.arange(devices, dtype=i32)[None, :]
     part = jnp.arange(4, dtype=i32)[:, None]
@@ -154,8 +164,8 @@
     before = jnp.sum(one_hot * exclusive[:, None, :], axis=2)
     arrival = (source_of * slot_rows + positions[None, :] - before)[:, :, None]
 
-    tile_shape = (2, block_rows, block_rows)
-    whole_tile = pl.BlockSpec(tile_shape, lambda j, *_: (0, 0, 0))
+    tile_shape = (block_rows, block_rows)
+    whole_tile = pl.BlockSpec(tile_shape, lambda j, *_: (0, 0))
     own, s1, s2, s3 = pl.pallas_call(
         partial(tiles_kernel, scaling=feat_width ** (-0.5)),
         out_shape=[jax.ShapeDtypeStruct(tile_shape, jnp.float32)]
@@ -172,7 +182,7 @@
         ),
         compiler_params=pltpu.CompilerParams(vmem_limit_bytes=VMEM_BYTES),
         name="compact_and_tiles",
-    )(mates, arrival, received)
+    )(edge[None], arrival, received)
 
     levels = devices.bit_length() - 1
     branches, keys = [], []
@@ -181,7 +191,9 @@
             branches.append(partial(exchange, 1 << a, 1 << b))
             keys.append((1 << a) | (1 << b))
     which = jnp.argmax(jnp.asarray(keys, dtype=i32) == (low | high)).astype(i32)
-    return lax.switch(which, branches, own, s1, s2, s3)
+    total, other = lax.switch(which, branches, own, s1, s2, s3)
+    mirrored = other.T.astype(jnp.float32)
+    return jnp.where((mates == edge)[:, None, None], total[None], mirrored[None])
 
 
 def solution(mesh):

time: 284 us -> 270 us (0.951)
  waiting for transfers between devices: 226 us -> 213 us
  Pallas kernels: 34.1 us -> 31.2 us
    ppermute x3, waiting for transfers between devices: 45.7 us -> 22.9 us  [exchange(): got = lax.ppermute(value, 'dev', [(d, d ^ mask) for d in range(devices)])]
    ppermute x0 -> x1, waiting for transfers between devices: none -> 9.17 us  [exchange(): lax.ppermute(total.astype(jnp.bfloat16), 'dev', [(d, d ^ owned_mask(d, lo...]
  transfers between devices with their start and end apart: 4 -> 5, of which waited for: 4 -> 4; matrix products, arithmetic and copies ran while one was open for 2% -> 2% of each run, Pallas kernels for 0% -> 0%
where the time goes in v1:
time: 270 us
  waiting for transfers between devices  213 us (79%)
  Pallas kernels  31.2 us (12%)
  starting transfers between devices  9.8 us (4%)
  other arithmetic  6.63 us (2%)
  local copies, waits for them, and re-layouts  5.28 us (2%)
  between operations  3.44 us (1%)
    all_to_all x1, waiting for transfers between devices, per_device(): lax.all_to_all(send, 'dev', split_axis=0, concat_axis=0, tiled=True)  181 us
    ppermute x3, waiting for transfers between devices, exchange(): got = lax.ppermute(value, 'dev', [(d, d ^ mask) for d in range(devices)])  22.9 us
    pallas_call x1, Pallas kernels, per_device(): pl.pallas_call(scatter_kernel, out_shape=jax.ShapeDtypeStruct((devices, 4...  21.4 us
    pallas_call x1, Pallas kernels, per_device(): pl.pallas_call(partial(tiles_kernel, scaling=feat_width ** (-0.5)), out_s...  9.74 us
    ppermute x1, waiting for transfers between devices, exchange(): lax.ppermute(total.astype(jnp.bfloat16), 'dev', [(d, d ^ owned_mask(d, lo...  9.17 us
    all_to_all x1, starting transfers between devices, per_device(): lax.all_to_all(send, 'dev', split_axis=0, concat_axis=0, tiled=True)  7.43 us
  transfers between devices with their start and end apart: 5, of which 4 were waited for; matrix products, arithmetic and copies ran while one was open for 2% of the time, Pallas kernels for 0%

profile of v1, /device:TPU:0, one launch (start us, length us, event | category | flops | bytes accessed | tf_op | source)
XLA Modules:
  0.0 269.7 jit_solution(17093316591346779105)
XLA Ops:
  0.0 1.3 fusion.12
  4.1 0.1 or.42.dest_ref
  4.2 0.1 xor.35
  4.3 0.7 dynamic-slice_bitcast_fusion
  5.1 1.3 select_n.105.picked_ref
  6.4 0.5 fusion.1.place_ref
  6.9 21.4 %condition_and_place.1 = bf16[32,4,32,1024]{3,2,1,0:T(8,128)(2,1)} custom-call(s32[128]{0:T(128)} %copy-done.1, s32[128]{0:T(128)} %fusion.1.place_ref, s32[1024,1]{1,0:T(8,128)} %select_n.105.picked_ref, bf16[1024,4096]{1,0:T(8,128)(2,1)} %rows_ref.1, bf16[8,512,512]{2,1,0:T(8,128)(2,1)} %factor_ref.1), custom_call_target="tpu_custom_call" | custom-call | tf_op jit(solution)/shard_map/condition_and_place/pallas_call | solution.py:132
  28.3 7.4 %all-to-all-start = ((bf16[32,4,32,1024]{3,2,1,0:T(8,128)(2,1)}), bf16[32,4,32,1024]{3,2,1,0:T(8,128)(2,1)}, u32[]{:S(2)}, u32[]{:S(2)}) async-start(bf16[32,4,32,1024]{3,2,1,0:T(8,128)(2,1)} %condition_and_place.1), calls=%async_computation | async-start | bytes 16777216 | tf_op jit(solution)/shard_map/all_to_all | solution.py:154
  35.9 0.1 fusion
  36.0 0.6 gather_fusion
  36.6 0.1 compare_and_fusion
  36.7 0.1 broadcast_select_fusion.1
  36.8 0.2 reduce_window_sum.11
  37.0 0.1 convert_reduce_fusion
  37.2 0.1 select_reduce_fusion
  37.3 0.4 copy.21
  37.7 0.4 copy.20
  38.1 1.1 sub.14.arrival_ref
  39.1 0.7 compare_reduce_fusion
  40.5 0.1 compare_reduce_fusion.1
  40.6 181.2 %all-to-all-done.received_ref = bf16[32,4,32,1024]{3,2,1,0:T(8,128)(2,1)} async-done(((bf16[32,4,32,1024]{3,2,1,0:T(8,128)(2,1)}), bf16[32,4,32,1024]{3,2,1,0:T(8,128)(2,1)}, u32[]{:S(2)}, u32[]{:S(2)}) %all-to-all-start) | async-done | bytes 8388640 | tf_op jit(solution)/shard_map/all_to_all | solution.py:154
  221.8 9.7 %compact_and_tiles.1 = (f32[512,512]{1,0:T(8,128)S(1)}, bf16[512,512]{1,0:T(8,128)(2,1)S(1)}, bf16[512,512]{1,0:T(8,128)(2,1)S(1)}, bf16[512,512]{1,0:T(8,128)(2,1)S(1)}) custom-call(s32[1]{0:T(128)} %bitcast.2.edge_ref, s32[4,512,1]{2,1,0:T(8,128)} %sub.14.arrival_ref, bf16[32,4,32,1024]{3,2,1,0:T(8,128)(2,1)} %all-to-all-done.received_ref), custom_call_target="tpu_custom_call" | custom-call | tf_op jit(solution)/shard_map/compact_and_tiles/pallas_call | solution.py:169
  231.6 34.9 %conditional.1 = (f32[512,512]{1,0:T(8,128)S(1)}, bf16[512,512]{1,0:T(8,128)(2,1)}) conditional(s32[]{:T(128)} %clamp.3, (bf16[512,512]{1,0:T(8,128)(2,1)S(1)}, f32[512,512]{1,0:T(8,128)S(1)}, bf16[512,512]{1,0:T(8,128)(2,1)S(1)}, bf16[512,512]{1,0:T(8,128)(2,1)S(1)}) %tuple.47, (bf16[512,512]{1,0:T(8,128)(2,1)S(1)}, ...), branch_computations={%region_4.5_spmd, %region_5.6_spmd, %region_6.7_spmd, %region_7.8_... | conditional | flops 1835008 | bytes 12583088 | solution.py:194
  231.8 2.0 collective-permute-start.14
  233.8 12.1 %collective-permute-done.12 = bf16[512,512]{1,0:T(8,128)(2,1)S(1)} collective-permute-done((bf16[512,512]{1,0:T(8,128)(2,1)S(1)}, bf16[512,512]{1,0:T(8,128)(2,1)S(1)}, u32[]{:S(2)}, u32[]{:S(2)}) %collective-permute-start.12) | collective-permute-done | bytes 524320 | tf_op jit(solution)/shard_map/cond/branch_3_fun/ppermute | solution.py:94
  245.9 10.8 %collective-permute-done.14 = bf16[512,512]{1,0:T(8,128)(2,1)S(1)} collective-permute-done((bf16[512,512]{1,0:T(8,128)(2,1)S(1)}, bf16[512,512]{1,0:T(8,128)(2,1)S(1)}, u32[]{:S(2)}, u32[]{:S(2)}) %collective-permute-start.14) | collective-permute-done | bytes 524320 | tf_op jit(solution)/shard_map/cond/branch_3_fun/ppermute | solution.py:94
  256.8 0.4 fusion.5
  257.1 0.2 collective-permute-start.15
  257.3 9.2 %collective-permute-done.15 = bf16[512,512]{1,0:T(8,128)(2,1)} collective-permute-done((bf16[512,512]{1,0:T(8,128)(2,1)S(1)}, bf16[512,512]{1,0:T(8,128)(2,1)}, u32[]{:S(2)}, u32[]{:S(2)}) %collective-permute-start.15) | collective-permute-done | bytes 524320 | tf_op jit(solution)/shard_map/cond/branch_3_fun/ppermute | solution.py:96
  266.5 1.2 convert_bitcast_fusion
  267.6 0.3 copy.23
  268.0 1.7 broadcast_select_fusion
  (21 shorter events, 0.5 us)
Async XLA Ops:
  4.2 2.7 %copy-start.1 = (s32[128]{0:T(128)}, s32[128]{0:T(128)S(1)}, u32[]{:S(2)}) copy-start(s32[128]{0:T(128)S(1)} %or.42.dest_ref) | copy-start | bytes 1540
  28.3 7.5 %copy-start = (s32[32,32]{1,0:T(8,128)S(1)}, s32[32,32]{1,0:T(8,128)}, u32[]{:S(2)}) copy-start(s32[32,32]{1,0:T(8,128)} %param.19) | copy-start | bytes 12292
  28.3 193.5 %all-to-all-start = ((bf16[32,4,32,1024]{3,2,1,0:T(8,128)(2,1)}), bf16[32,4,32,1024]{3,2,1,0:T(8,128)(2,1)}, u32[]{:S(2)}, u32[]{:S(2)}) async-start(bf16[32,4,32,1024]{3,2,1,0:T(8,128)(2,1)} %condition_and_place.1), calls=%async_computation | async-start | bytes 16777216 | tf_op jit(solution)/shard_map/all_to_all | solution.py:154
  35.8 3.4 %copy-start.3 = (s32[10]{0:T(128)S(1)}, s32[10]{0:T(128)}, u32[]{:S(2)}) copy-start(s32[10]{0:T(128)} %constant.60.clone) | copy-start | bytes 124
  35.8 4.7 %copy-start.2 = (s32[2,32]{1,0:T(2,128)S(1)}, s32[2,32]{1,0:T(2,128)}, u32[]{:S(2)}) copy-start(s32[2,32]{1,0:T(2,128)} %param.20) | copy-start | bytes 772
  231.6 14.3 %collective-permute-start.12 = (bf16[512,512]{1,0:T(8,128)(2,1)S(1)}, bf16[512,512]{1,0:T(8,128)(2,1)S(1)}, u32[]{:S(2)}, u32[]{:S(2)}) collective-permute-start(bf16[512,512]{1,0:T(8,128)(2,1)S(1)} %get-tuple-element.98), channel_id=1, source_target_pairs={{0,9},{1,8},{2,11},{3,10},{4,13},{5,12},{6,15},{7,14},{8,1},{9,0},... | collective-permute-start | bytes 1572872 | tf_op jit(solution)/shard_map/cond/branch_3_fun/ppermute | solution.py:94
  231.7 14.2 %collective-permute-start.13 = (bf16[512,512]{1,0:T(8,128)(2,1)S(1)}, bf16[512,512]{1,0:T(8,128)(2,1)S(1)}, u32[]{:S(2)}, u32[]{:S(2)}) collective-permute-start(bf16[512,512]{1,0:T(8,128)(2,1)S(1)} %get-tuple-element.99), channel_id=1, source_target_pairs={{0,1},{1,0},{2,3},{3,2},{4,5},{5,4},{6,7},{7,6},{8,9},{9,8},{10,11... | collective-permute-start | bytes 1572872 | tf_op jit(solution)/shard_map/cond/branch_3_fun/ppermute | solution.py:94
  231.8 25.0 %collective-permute-start.14 = (bf16[512,512]{1,0:T(8,128)(2,1)S(1)}, bf16[512,512]{1,0:T(8,128)(2,1)S(1)}, u32[]{:S(2)}, u32[]{:S(2)}) collective-permute-start(bf16[512,512]{1,0:T(8,128)(2,1)S(1)} %get-tuple-element.100), channel_id=1, source_target_pairs={{0,8},{1,9},{2,10},{3,11},{4,12},{5,13},{6,14},{7,15},{8,0},{9,1},... | collective-permute-start | bytes 1572872 | tf_op jit(solution)/shard_map/cond/branch_3_fun/ppermute | solution.py:94
  257.1 9.3 %collective-permute-start.15 = (bf16[512,512]{1,0:T(8,128)(2,1)S(1)}, bf16[512,512]{1,0:T(8,128)(2,1)}, u32[]{:S(2)}, u32[]{:S(2)}) collective-permute-start(bf16[512,512]{1,0:T(8,128)(2,1)S(1)} %get-tuple-element.145), channel_id=1, source_target_pairs={{0,1},{1,9},{2,3},{3,11},{4,5},{5,13},{6,7},{7,15},{8,0},{9,8},{10... | collective-permute-start | bytes 1572872 | tf_op jit(solution)/shard_map/cond/branch_3_fun/ppermute | solution.py:96

commit v2 on v1

--- a/solution.py
+++ b/solution.py
@@ -13,15 +13,12 @@
 def scatter_kernel(
     dest_ref, place_ref, picked_ref, rows_ref, factor_ref, out_ref, select, stage, sem
 ):
-    layer = pl.program_id(0)
-    layers = pl.num_programs(0)
+    part = pl.program_id(0)
+    parts = pl.num_programs(0)
     players, slot_rows, width = stage.shape[1:]
-    capacity = rows_ref.shape[0]
-    per_part = layers // 4
-    part = layer // per_part
-    buf = lax.rem(layer, 2)
-
-    @pl.when(layer == 0)
+    buf = lax.rem(part, 2)
+
+    @pl.when(part == 0)
     def _():
         lanes = lax.broadcasted_iota(jnp.int32, select.shape, 1)
         select[...] = (lanes == picked_ref[...]).astype(jnp.float32).astype(jnp.bfloat16)
@@ -33,30 +30,32 @@
     def drain(which):
         pltpu.make_async_copy(stage.at[which], stage.at[which], sem.at[which]).wait()
 
-    @pl.when(layer >= 2)
+    @pl.when(part >= 2)
     def _():
         drain(buf)
 
     moved = jnp.dot(select[...], conditioned, preferred_element_type=jnp.float32)
     stage[buf] = moved.reshape(players, slot_rows, width).astype(jnp.bfloat16)
-    column = pl.multiple_of(lax.rem(layer, per_part) * width, width)
 
     @pl.loop(0, players)
     def _(player):
         at = part * players + player
         pltpu.make_async_copy(
             stage.at[buf, player],
-            out_ref.at[dest_ref[at], place_ref[at], :, pl.ds(column, width)],
+            out_ref.at[dest_ref[at], place_ref[at]],
             sem.at[buf],
         ).start()
 
-    @pl.when(layer == layers - 1)
+    @pl.when(part == parts - 1)
     def _():
         drain(1 - buf)
         drain(buf)
 
 
-def tiles_kernel(edge_ref, arrival_ref, received_ref, own_ref, s1_ref, s2_ref, s3_ref, blocks, *, scaling):
+def tiles_kernel(edge_ref, arrival_ref, received_ref, *refs, scaling, first, last):
+    outs, blocks = refs[:-1], refs[-1]
+    if not first:
+        sum_ref, outs = outs[0], outs[1:]
     step = pl.program_id(0)
     sources, _, slot_rows, width = received_ref.shape
     rows = arrival_ref.shape[1]
@@ -77,10 +76,15 @@
     @pl.when(step == 3)
     def _():
         edge = edge_ref[0]
-        own_ref[...] = tile(0, edge) * scaling
-        s1_ref[...] = (tile(1, 1 ^ (3 - edge)) * scaling).astype(jnp.bfloat16)
-        s2_ref[...] = (tile(2, 2 ^ (3 - edge)) * scaling).astype(jnp.bfloat16)
-        s3_ref[...] = (tile(3, 3 ^ edge) * scaling).astype(jnp.bfloat16)
+        mates = (edge, 1 ^ (3 - edge), 2 ^ (3 - edge), 3 ^ edge)
+        for player, mate in enumerate(mates):
+            total = tile(player, mate)
+            if not first:
+                total = total + sum_ref[player]
+            if last:
+                outs[player][...] = (total * scaling).astype(outs[player].dtype)
+            else:
+                outs[0][player] = total
 
 
 def owned_mask(device, low, high):
@@ -108,7 +112,7 @@
     layers, width, _ = factor.shape
     slot_rows = capacity // devices
     block_rows = capacity // 2
-    part_width = feat_width // 4
+    per_part = layers // 4
     i32 = jnp.int32
 
     low = jnp.minimum(partners[0, 0], partners[1, 0])
@@ -129,29 +133,39 @@
     usable = offsets[None, :] < count_row[:, None]
     picked = jnp.where(usable, start_row[:, None] + offsets[None, :], -1).reshape(-1, 1)
 
-    send = pl.pallas_call(
-        scatter_kernel,
-        out_shape=jax.ShapeDtypeStruct((devices, 4, slot_rows, part_width), jnp.bfloat16),
-        grid_spec=pltpu.PrefetchScalarGridSpec(
-            num_scalar_prefetch=2,
-            grid=(layers,),
-            in_specs=[
-                pl.BlockSpec((capacity, 1), lambda l, *_: (0, 0)),
-                pl.BlockSpec((capacity, width), lambda l, *_: (0, l)),
-                pl.BlockSpec((1, width, width), lambda l, *_: (l, 0, 0)),
-            ],
-            out_specs=pl.BlockSpec(memory_space=pl.ANY),
-            scratch_shapes=[
-                pltpu.VMEM((capacity, capacity), jnp.bfloat16),
-                pltpu.VMEM((2, devices, slot_rows, width), jnp.bfloat16),
-                pltpu.SemaphoreType.DMA((2,)),
-            ],
-        ),
-        compiler_params=pltpu.CompilerParams(vmem_limit_bytes=VMEM_BYTES),
-        name="condition_and_place",
-    )(dest, place, picked, source_rows, factor)
-
-    received = lax.all_to_all(send, "dev", split_axis=0, concat_axis=0, tiled=True)
+    sent = []
+    for chunk in range(per_part):
+        layer_of = partial(lambda chunk, p: p * per_part + chunk, chunk)
+        sent.append(pl.pallas_call(
+            scatter_kernel,
+            out_shape=jax.ShapeDtypeStruct((devices, 4, slot_rows, width), jnp.bfloat16),
+            grid_spec=pltpu.PrefetchScalarGridSpec(
+                num_scalar_prefetch=2,
+                grid=(4,),
+                in_specs=[
+                    pl.BlockSpec((capacity, 1), lambda p, *_: (0, 0)),
+                    pl.BlockSpec((capacity, width), lambda p, *_, f=layer_of: (0, f(p))),
+                    pl.BlockSpec((1, width, width), lambda p, *_, f=layer_of: (f(p), 0, 0)),
+                ],
+                out_specs=pl.BlockSpec(memory_space=pl.ANY),
+                scratch_shapes=[
+                    pltpu.VMEM((capacity, capacity), jnp.bfloat16),
+                    pltpu.VMEM((2, devices, slot_rows, width), jnp.bfloat16),
+                    pltpu.SemaphoreType.DMA((2,)),
+                ],
+            ),
+            compiler_params=pltpu.CompilerParams(vmem_limit_bytes=VMEM_BYTES),
+            cost_estimate=pl.CostEstimate(
+                flops=8 * capacity * width * (width + capacity),
+                bytes_accessed=16 * capacity * width + 8 * width * width,
+                transcendentals=0,
+            ),
+            name=f"condition_and_place_{chunk}",
+        )(dest, place, picked, source_rows, factor))
+
+    received = [
+        lax.all_to_all(send, "dev", split_axis=0, concat_axis=0, tiled=True) for send in sent
+    ]
 
     combos = jnp.stack([jnp.zeros_like(low), low, high, low | high])
     counts = jnp.take(plan_count, own_index ^ combos, axis=1).T
@@ -166,23 +180,38 @@
 
     tile_shape = (block_rows, block_rows)
     whole_tile = pl.BlockSpec(tile_shape, lambda j, *_: (0, 0))
-    own, s1, s2, s3 = pl.pallas_call(
-        partial(tiles_kernel, scaling=feat_width ** (-0.5)),
-        out_shape=[jax.ShapeDtypeStruct(tile_shape, jnp.float32)]
-        + [jax.ShapeDtypeStruct(tile_shape, jnp.bfloat16)] * 3,
-        grid_spec=pltpu.PrefetchScalarGridSpec(
-            num_scalar_prefetch=1,
-            grid=(4,),
-            in_specs=[
-                pl.BlockSpec((1, block_rows, 1), lambda j, *_: (j, 0, 0)),
-                pl.BlockSpec((devices, 1, slot_rows, part_width), lambda j, *_: (0, j, 0, 0)),
-            ],
-            out_specs=[whole_tile] * 4,
-            scratch_shapes=[pltpu.VMEM((4, block_rows, part_width), jnp.bfloat16)],
-        ),
-        compiler_params=pltpu.CompilerParams(vmem_limit_bytes=VMEM_BYTES),
-        name="compact_and_tiles",
-    )(edge[None], arrival, received)
+    sums_shape = jax.ShapeDtypeStruct((4,) + tile_shape, jnp.float32)
+    sums_spec = pl.BlockSpec((4,) + tile_shape, lambda j, *_: (0, 0, 0))
+    sums = []
+    for chunk in range(per_part):
+        last = chunk == per_part - 1
+        out_shape, out_specs = [sums_shape], [sums_spec]
+        if last:
+            out_shape = [jax.ShapeDtypeStruct(tile_shape, jnp.float32)]
+            out_shape += [jax.ShapeDtypeStruct(tile_shape, jnp.bfloat16)] * 3
+            out_specs = [whole_tile] * 4
+        sums = pl.pallas_call(
+            partial(tiles_kernel, scaling=feat_width ** (-0.5), first=chunk == 0, last=last),
+            out_shape=out_shape,
+            grid_spec=pltpu.PrefetchScalarGridSpec(
+                num_scalar_prefetch=1,
+                grid=(4,),
+                in_specs=[
+                    pl.BlockSpec((1, block_rows, 1), lambda j, *_: (j, 0, 0)),
+                    pl.BlockSpec((devices, 1, slot_rows, width), lambda j, *_: (0, j, 0, 0)),
+                ] + [sums_spec] * len(sums),
+                out_specs=out_specs,
+                scratch_shapes=[pltpu.VMEM((4, block_rows, width), jnp.bfloat16)],
+            ),
+            compiler_params=pltpu.CompilerParams(vmem_limit_bytes=VMEM_BYTES),
+            cost_estimate=pl.CostEstimate(
+                flops=8 * block_rows * width * (capacity + block_rows),
+                bytes_accessed=8 * capacity * width + 16 * block_rows * block_rows,
+                transcendentals=0,
+            ),
+            name=f"compact_and_tiles_{chunk}",
+        )(edge[None], arrival, received[chunk], *sums)
+    own, s1, s2, s3 = sums
 
     levels = devices.bit_length() - 1
     branches, keys = [], []

time: 270 us -> 267 us (0.989)
  waiting for transfers between devices: 213 us -> 197 us
  Pallas kernels: 31.2 us -> 40.4 us
  starting transfers between devices: 9.8 us -> 16.7 us
    all_to_all x1 -> x2, waiting for transfers between devices: 181 us -> 163 us  [per_device(): lax.all_to_all(send, 'dev', split_axis=0, concat_axis=0, tiled=True)]
    pallas_call x1 -> x2, Pallas kernels: 9.74 us -> 15.8 us  [per_device(): pl.pallas_call(partial(tiles_kernel, scaling=feat_width ** (-0.5), first=...]
    all_to_all x1 -> x2, starting transfers between devices: 7.43 us -> 11.5 us  [per_device(): lax.all_to_all(send, 'dev', split_axis=0, concat_axis=0, tiled=True)]
    ppermute x1, waiting for transfers between devices: 9.17 us -> 12.4 us  [exchange(): lax.ppermute(total.astype(jnp.bfloat16), 'dev', [(d, d ^ owned_mask(d, lo...]
    pallas_call x1 -> x2, Pallas kernels: 21.4 us -> 24.6 us  [per_device(): pl.pallas_call(scatter_kernel, out_shape=jax.ShapeDtypeStruct((devices, 4...]
  transfers between devices with their start and end apart: 5 -> 6, of which waited for: 4 -> 6; matrix products, arithmetic and copies ran while one was open for 2% -> 2% of each run, Pallas kernels for 0% -> 8%
where the time goes in v2:
time: 267 us; the launch traced here: 269 us
  waiting for transfers between devices  197 us (74%)
  Pallas kernels  40.4 us (15%)
  starting transfers between devices  16.7 us (6%)
  other arithmetic  6.63 us (2%)
  local copies, waits for them, and re-layouts  5.22 us (2%)
  between operations  3.18 us (1%)
    all_to_all x2, waiting for transfers between devices, per_device(): lax.all_to_all(send, 'dev', split_axis=0, concat_axis=0, tiled=True)  163 us
    pallas_call x2, Pallas kernels, per_device(): pl.pallas_call(scatter_kernel, out_shape=jax.ShapeDtypeStruct((devices, 4...  24.6 us
    ppermute x3, waiting for transfers between devices, exchange(): got = lax.ppermute(value, 'dev', [(d, d ^ mask) for d in range(devices)])  22.1 us
    pallas_call x2, Pallas kernels, per_device(): pl.pallas_call(partial(tiles_kernel, scaling=feat_width ** (-0.5), first=...  15.8 us
    ppermute x1, waiting for transfers between devices, exchange(): lax.ppermute(total.astype(jnp.bfloat16), 'dev', [(d, d ^ owned_mask(d, lo...  12.4 us
    all_to_all x2, starting transfers between devices, per_device(): lax.all_to_all(send, 'dev', split_axis=0, concat_axis=0, tiled=True)  11.5 us
  transfers between devices with their start and end apart: 6, of which 6 were waited for; matrix products, arithmetic and copies ran while one was open for 2% of the time, Pallas kernels for 8%

profile of v2, /device:TPU:0, one launch (start us, length us, event | category | flops | bytes accessed | tf_op | source)
XLA Modules:
  0.0 269.2 jit_solution(13134341922134939528)
XLA Ops:
  0.0 1.3 fusion.12
  4.0 0.7 dynamic-slice_bitcast_fusion
  4.8 1.3 select_n.105.picked_ref
  6.1 0.5 fusion.1.place_ref
  6.7 12.3 %condition_and_place_0.1 = bf16[32,4,32,512]{3,2,1,0:T(8,128)(2,1)} custom-call(s32[128]{0:T(128)} %copy-done.2, s32[128]{0:T(128)} %fusion.1.place_ref, s32[1024,1]{1,0:T(8,128)} %select_n.105.picked_ref, bf16[1024,4096]{1,0:T(8,128)(2,1)} %rows_ref.3, bf16[8,512,512]{2,1,0:T(8,128)(2,1)} %factor_ref.3), custom_call_target="tpu_custom_call" | custom-call | flops 6442450944 | bytes 10485760 | tf_op jit(solution)/shard_map/condition_and_place_0/pallas_call | solution.py:139
  19.0 7.4 %all-to-all-start.1 = ((bf16[32,4,32,512]{3,2,1,0:T(8,128)(2,1)}), bf16[32,4,32,512]{3,2,1,0:T(8,128)(2,1)}, u32[]{:S(2)}, u32[]{:S(2)}) async-start(bf16[32,4,32,512]{3,2,1,0:T(8,128)(2,1)} %condition_and_place_0.1), calls=%async_computation.1 | async-start | bytes 8388608 | tf_op jit(solution)/shard_map/all_to_all | solution.py:167
  26.4 12.3 %condition_and_place_1.1 = bf16[32,4,32,512]{3,2,1,0:T(8,128)(2,1)} custom-call(s32[128]{0:T(128)} %copy-done.2, s32[128]{0:T(128)} %fusion.1.place_ref, s32[1024,1]{1,0:T(8,128)} %select_n.105.picked_ref, bf16[1024,4096]{1,0:T(8,128)(2,1)} %rows_ref.3, bf16[8,512,512]{2,1,0:T(8,128)(2,1)} %factor_ref.3), custom_call_target="tpu_custom_call" | custom-call | flops 6442450944 | bytes 10485760 | tf_op jit(solution)/shard_map/condition_and_place_1/pallas_call | solution.py:139
  38.7 81.6 %all-to-all-done.1.received_ref = bf16[32,4,32,512]{3,2,1,0:T(8,128)(2,1)} async-done(((bf16[32,4,32,512]{3,2,1,0:T(8,128)(2,1)}), bf16[32,4,32,512]{3,2,1,0:T(8,128)(2,1)}, u32[]{:S(2)}, u32[]{:S(2)}) %all-to-all-start.1) | async-done | bytes 4194336 | tf_op jit(solution)/shard_map/all_to_all | solution.py:167
  120.3 4.1 %all-to-all-start = ((bf16[32,4,32,512]{3,2,1,0:T(8,128)(2,1)}), bf16[32,4,32,512]{3,2,1,0:T(8,128)(2,1)}, u32[]{:S(2)}, u32[]{:S(2)}) async-start(bf16[32,4,32,512]{3,2,1,0:T(8,128)(2,1)} %condition_and_place_1.1), calls=%async_computation | async-start | bytes 8388608 | tf_op jit(solution)/shard_map/all_to_all | solution.py:167
  124.5 0.1 fusion
  124.6 0.6 gather_fusion
  125.3 0.2 reduce_window_sum.11
  125.9 0.4 copy.23
  126.3 0.4 copy.22
  126.6 0.7 compare_reduce_fusion
  127.9 1.1 sub.14.arrival_ref
  129.1 8.2 %compact_and_tiles_0.1.refs_0_ = f32[4,512,512]{2,1,0:T(8,128)} custom-call(s32[1]{0:T(128)} %bitcast.2.edge_ref, s32[4,512,1]{2,1,0:T(8,128)} %sub.14.arrival_ref, bf16[32,4,32,512]{3,2,1,0:T(8,128)(2,1)} %all-to-all-done.1.received_ref), custom_call_target="tpu_custom_call" | custom-call | flops 3221225472 | bytes 8388608 | tf_op jit(solution)/shard_map/compact_and_tiles_0/pallas_call | solution.py:193
  137.3 80.9 %all-to-all-done.received_ref = bf16[32,4,32,512]{3,2,1,0:T(8,128)(2,1)} async-done(((bf16[32,4,32,512]{3,2,1,0:T(8,128)(2,1)}), bf16[32,4,32,512]{3,2,1,0:T(8,128)(2,1)}, u32[]{:S(2)}, u32[]{:S(2)}) %all-to-all-start) | async-done | bytes 4194336 | tf_op jit(solution)/shard_map/all_to_all | solution.py:167
  218.3 7.6 %compact_and_tiles_1.1 = (f32[512,512]{1,0:T(8,128)S(1)}, bf16[512,512]{1,0:T(8,128)(2,1)S(1)}, bf16[512,512]{1,0:T(8,128)(2,1)S(1)}, bf16[512,512]{1,0:T(8,128)(2,1)S(1)}) custom-call(s32[1]{0:T(128)} %bitcast.2.edge_ref, s32[4,512,1]{2,1,0:T(8,128)} %sub.14.arrival_ref, bf16[32,4,32,512]{3,2,1,0:T(8,128)(2,1)} %all-to-all-done.received_ref, ...), custom_call_target="tpu_custom_call" | custom-call | flops 3221225472 | bytes 8388608 | tf_op jit(solution)/shard_map/compact_and_tiles_1/pallas_call | solution.py:193
  225.9 40.1 %conditional.1 = (f32[512,512]{1,0:T(8,128)S(1)}, bf16[512,512]{1,0:T(8,128)(2,1)}) conditional(s32[]{:T(128)} %clamp.3, (bf16[512,512]{1,0:T(8,128)(2,1)S(1)}, f32[512,512]{1,0:T(8,128)S(1)}, bf16[512,512]{1,0:T(8,128)(2,1)S(1)}, bf16[512,512]{1,0:T(8,128)(2,1)S(1)}) %tuple.47, (bf16[512,512]{1,0:T(8,128)(2,1)S(1)}, ...), branch_computations={%region_4.5_spmd, %region_5.6_spmd, %region_6.7_spmd, %region_7.8_... | conditional | flops 1835008 | bytes 12583088 | solution.py:223
  225.9 2.5 collective-permute-start.8
  228.4 0.3 collective-permute-start.9
  228.7 0.8 collective-permute-start.10
  229.5 12.3 %collective-permute-done.8 = bf16[512,512]{1,0:T(8,128)(2,1)S(1)} collective-permute-done((bf16[512,512]{1,0:T(8,128)(2,1)S(1)}, bf16[512,512]{1,0:T(8,128)(2,1)S(1)}, u32[]{:S(2)}, u32[]{:S(2)}) %collective-permute-start.8) | collective-permute-done | bytes 524320 | tf_op jit(solution)/shard_map/cond/branch_2_fun/ppermute | solution.py:98
  241.8 9.6 %collective-permute-done.9 = bf16[512,512]{1,0:T(8,128)(2,1)S(1)} collective-permute-done((bf16[512,512]{1,0:T(8,128)(2,1)S(1)}, bf16[512,512]{1,0:T(8,128)(2,1)S(1)}, u32[]{:S(2)}, u32[]{:S(2)}) %collective-permute-start.9) | collective-permute-done | bytes 524320 | tf_op jit(solution)/shard_map/cond/branch_2_fun/ppermute | solution.py:98
  251.4 0.2 collective-permute-done.10
  251.6 0.4 fusion.4
  251.9 1.6 collective-permute-start.11
  253.6 12.4 %collective-permute-done.11 = bf16[512,512]{1,0:T(8,128)(2,1)} collective-permute-done((bf16[512,512]{1,0:T(8,128)(2,1)S(1)}, bf16[512,512]{1,0:T(8,128)(2,1)}, u32[]{:S(2)}, u32[]{:S(2)}) %collective-permute-start.11) | collective-permute-done | bytes 524320 | tf_op jit(solution)/shard_map/cond/branch_2_fun/ppermute | solution.py:100
  265.9 1.2 convert_bitcast_fusion
  267.1 0.3 copy.26
  267.5 1.7 broadcast_select_fusion
  (25 shorter events, 1.0 us)
Async XLA Ops:
  3.9 2.8 %copy-start.2 = (s32[128]{0:T(128)}, s32[128]{0:T(128)S(1)}, u32[]{:S(2)}) copy-start(s32[128]{0:T(128)S(1)} %or.42.dest_ref) | copy-start | bytes 1540
  19.0 101.3 %all-to-all-start.1 = ((bf16[32,4,32,512]{3,2,1,0:T(8,128)(2,1)}), bf16[32,4,32,512]{3,2,1,0:T(8,128)(2,1)}, u32[]{:S(2)}, u32[]{:S(2)}) async-start(bf16[32,4,32,512]{3,2,1,0:T(8,128)(2,1)} %condition_and_place_0.1), calls=%async_computation.1 | async-start | bytes 8388608 | tf_op jit(solution)/shard_map/all_to_all | solution.py:167
  38.7 85.7 %copy-start = (s32[32,32]{1,0:T(8,128)S(1)}, s32[32,32]{1,0:T(8,128)}, u32[]{:S(2)}) copy-start(s32[32,32]{1,0:T(8,128)} %param.19) | copy-start | bytes 12292
  38.7 87.9 %copy-start.3 = (s32[10]{0:T(128)S(1)}, s32[10]{0:T(128)}, u32[]{:S(2)}) copy-start(s32[10]{0:T(128)} %constant.60.clone) | copy-start | bytes 124
  120.3 98.0 %all-to-all-start = ((bf16[32,4,32,512]{3,2,1,0:T(8,128)(2,1)}), bf16[32,4,32,512]{3,2,1,0:T(8,128)(2,1)}, u32[]{:S(2)}, u32[]{:S(2)}) async-start(bf16[32,4,32,512]{3,2,1,0:T(8,128)(2,1)} %condition_and_place_1.1), calls=%async_computation | async-start | bytes 8388608 | tf_op jit(solution)/shard_map/all_to_all | solution.py:167
  124.4 4.6 %copy-start.1 = (s32[2,32]{1,0:T(2,128)S(1)}, s32[2,32]{1,0:T(2,128)}, u32[]{:S(2)}) copy-start(s32[2,32]{1,0:T(2,128)} %param.20) | copy-start | bytes 772
  225.9 15.8 %collective-permute-start.8 = (bf16[512,512]{1,0:T(8,128)(2,1)S(1)}, bf16[512,512]{1,0:T(8,128)(2,1)S(1)}, u32[]{:S(2)}, u32[]{:S(2)}) collective-permute-start(bf16[512,512]{1,0:T(8,128)(2,1)S(1)} %get-tuple-element.94), channel_id=1, source_target_pairs={{0,6},{1,7},{2,4},{3,5},{4,2},{5,3},{6,0},{7,1},{8,14},{9,15},{10,... | collective-permute-start | bytes 1572872 | tf_op jit(solution)/shard_map/cond/branch_2_fun/ppermute | solution.py:98
  228.4 23.0 %collective-permute-start.9 = (bf16[512,512]{1,0:T(8,128)(2,1)S(1)}, bf16[512,512]{1,0:T(8,128)(2,1)S(1)}, u32[]{:S(2)}, u32[]{:S(2)}) collective-permute-start(bf16[512,512]{1,0:T(8,128)(2,1)S(1)} %get-tuple-element.95), channel_id=1, source_target_pairs={{0,2},{1,3},{2,0},{3,1},{4,6},{5,7},{6,4},{7,5},{8,10},{9,11},{10,... | collective-permute-start | bytes 1572872 | tf_op jit(solution)/shard_map/cond/branch_2_fun/ppermute | solution.py:98
  228.7 22.9 %collective-permute-start.10 = (bf16[512,512]{1,0:T(8,128)(2,1)S(1)}, bf16[512,512]{1,0:T(8,128)(2,1)S(1)}, u32[]{:S(2)}, u32[]{:S(2)}) collective-permute-start(bf16[512,512]{1,0:T(8,128)(2,1)S(1)} %get-tuple-element.96), channel_id=1, source_target_pairs={{0,4},{1,5},{2,6},{3,7},{4,0},{5,1},{6,2},{7,3},{8,12},{9,13},{10,... | collective-permute-start | bytes 1572872 | tf_op jit(solution)/shard_map/cond/branch_2_fun/ppermute | solution.py:98
  251.9 14.0 %collective-permute-start.11 = (bf16[512,512]{1,0:T(8,128)(2,1)S(1)}, bf16[512,512]{1,0:T(8,128)(2,1)}, u32[]{:S(2)}, u32[]{:S(2)}) collective-permute-start(bf16[512,512]{1,0:T(8,128)(2,1)S(1)} %get-tuple-element.143), channel_id=1, source_target_pairs={{0,2},{1,3},{2,6},{3,7},{4,0},{5,1},{6,4},{7,5},{8,10},{9,11},{10,... | collective-permute-start | bytes 1572872 | tf_op jit(solution)/shard_map/cond/branch_2_fun/ppermute | solution.py:100

commit v3 on v2

--- a/solution.py
+++ b/solution.py
@@ -11,7 +11,7 @@
 
 
 def scatter_kernel(
-    dest_ref, place_ref, picked_ref, rows_ref, factor_ref, out_ref, select, stage, sem
+    own_ref, partners_ref, start_ref, count_ref, rows_ref, factor_ref, out_ref, picked, select, stage, sem
 ):
     part = pl.program_id(0)
     parts = pl.num_programs(0)
@@ -20,8 +20,16 @@
 
     @pl.when(part == 0)
     def _():
+        offsets = lax.broadcasted_iota(jnp.int32, (slot_rows, picked.shape[1]), 0)
+
+        @pl.loop(0, players)
+        def _(player):
+            start, count = start_ref[own_ref[0], player], count_ref[own_ref[0], player]
+            slot = pl.ds(pl.multiple_of(player * slot_rows, slot_rows), slot_rows)
+            picked[slot, :] = jnp.where(offsets < count, start + offsets, -1)
+
         lanes = lax.broadcasted_iota(jnp.int32, select.shape, 1)
-        select[...] = (lanes == picked_ref[...]).astype(jnp.float32).astype(jnp.bfloat16)
+        select[...] = (lanes == picked[:, :1]).astype(jnp.float32).astype(jnp.bfloat16)
 
     conditioned = jnp.dot(
         rows_ref[...], factor_ref[0], preferred_element_type=jnp.float32
@@ -37,12 +45,18 @@
     moved = jnp.dot(select[...], conditioned, preferred_element_type=jnp.float32)
     stage[buf] = moved.reshape(players, slot_rows, width).astype(jnp.bfloat16)
 
+    low = jnp.minimum(partners_ref[0, 0], partners_ref[1, 0])
+    high = jnp.maximum(partners_ref[0, 0], partners_ref[1, 0])
+    bits = jnp.where((part & 1) != 0, low, 0) | jnp.where((part & 2) != 0, high, 0)
+
     @pl.loop(0, players)
     def _(player):
-        at = part * players + player
+        dest = (player & ~(low | high)) | bits
+        differs = player ^ dest
+        place = jnp.where((differs & low) != 0, 1, 0) + jnp.where((differs & high) != 0, 2, 0)
         pltpu.make_async_copy(
             stage.at[buf, player],
-            out_ref.at[dest_ref[at], place_ref[at]],
+            out_ref.at[dest, place],
             sem.at[buf],
         ).start()
 
@@ -120,19 +134,6 @@
     mates = jnp.where(partners[:, 0] == low, 1, 2).astype(i32)
     edge = jnp.where(((own_index & low) != 0) == ((own_index & high) != 0), 1, 2).astype(i32)
 
-    player = jnp.arange(devices, dtype=i32)[None, :]
-    part = jnp.arange(4, dtype=i32)[:, None]
-    dest = (player & ~low & ~high) | jnp.where(part & 1, low, 0) | jnp.where(part & 2, high, 0)
-    differs = player ^ dest
-    place = jnp.where(differs & low, 1, 0) + jnp.where(differs & high, 2, 0)
-    dest, place = dest.reshape(-1).astype(i32), place.reshape(-1).astype(i32)
-
-    start_row = lax.dynamic_index_in_dim(plan_start, own_index, 0, keepdims=False)
-    count_row = lax.dynamic_index_in_dim(plan_count, own_index, 0, keepdims=False)
-    offsets = jnp.arange(slot_rows, dtype=i32)
-    usable = offsets[None, :] < count_row[:, None]
-    picked = jnp.where(usable, start_row[:, None] + offsets[None, :], -1).reshape(-1, 1)
-
     sent = []
     for chunk in range(per_part):
         layer_of = partial(lambda chunk, p: p * per_part + chunk, chunk)
@@ -140,15 +141,15 @@
             scatter_kernel,
             out_shape=jax.ShapeDtypeStruct((devices, 4, slot_rows, width), jnp.bfloat16),
             grid_spec=pltpu.PrefetchScalarGridSpec(
-                num_scalar_prefetch=2,
+                num_scalar_prefetch=4,
                 grid=(4,),
                 in_specs=[
-                    pl.BlockSpec((capacity, 1), lambda p, *_: (0, 0)),
                     pl.BlockSpec((capacity, width), lambda p, *_, f=layer_of: (0, f(p))),
                     pl.BlockSpec((1, width, width), lambda p, *_, f=layer_of: (f(p), 0, 0)),
                 ],
                 out_specs=pl.BlockSpec(memory_space=pl.ANY),
                 scratch_shapes=[
+                    pltpu.VMEM((capacity, 128), jnp.int32),
                     pltpu.VMEM((capacity, capacity), jnp.bfloat16),
                     pltpu.VMEM((2, devices, slot_rows, width), jnp.bfloat16),
                     pltpu.SemaphoreType.DMA((2,)),
@@ -161,7 +162,7 @@
                 transcendentals=0,
             ),
             name=f"condition_and_place_{chunk}",
-        )(dest, place, picked, source_rows, factor))
+        )(own_index[None], partners, plan_start, plan_count, source_rows, factor))
 
     received = [
         lax.all_to_all(send, "dev", split_axis=0, concat_axis=0, tiled=True) for send in sent

time: 267 us -> 261 us (0.978); the launches traced: 269 us -> 258 us
  waiting for transfers between devices: 197 us -> 190 us
  local copies, waits for them, and re-layouts: 5.22 us -> 2.31 us
  starting transfers between devices: 16.7 us -> 13.9 us
    all_to_all x2, waiting for transfers between devices: 163 us -> 158 us  [per_device(): lax.all_to_all(send, 'dev', split_axis=0, concat_axis=0, tiled=True)]
    ppermute x1, waiting for transfers between devices: 12.4 us -> 9.17 us  [exchange(): lax.ppermute(total.astype(jnp.bfloat16), 'dev', [(d, d ^ owned_mask(d, lo...]
  transfers between devices with their start and end apart: 6 -> 6, of which waited for: 6 -> 5; matrix products, arithmetic and copies ran while one was open for 2% -> 2% of each run, Pallas kernels for 8% -> 8%
where the time goes in v3:
time: 261 us; the launch traced here: 258 us
  waiting for transfers between devices  190 us (73%)
  Pallas kernels  42.3 us (16%)
  starting transfers between devices  13.9 us (5%)
  other arithmetic  5.89 us (2%)
  between operations  3.44 us (1%)
    all_to_all x2, waiting for transfers between devices, per_device(): lax.all_to_all(send, 'dev', split_axis=0, concat_axis=0, tiled=True)  158 us
    pallas_call x2, Pallas kernels, per_device(): pl.pallas_call(scatter_kernel, out_shape=jax.ShapeDtypeStruct((devices, 4...  26.4 us
    ppermute x3, waiting for transfers between devices, exchange(): got = lax.ppermute(value, 'dev', [(d, d ^ mask) for d in range(devices)])  23 us
    pallas_call x2, Pallas kernels, per_device(): pl.pallas_call(partial(tiles_kernel, scaling=feat_width ** (-0.5), first=...  15.8 us
    all_to_all x2, starting transfers between devices, per_device(): lax.all_to_all(send, 'dev', split_axis=0, concat_axis=0, tiled=True)  11.5 us
    ppermute x1, waiting for transfers between devices, exchange(): lax.ppermute(total.astype(jnp.bfloat16), 'dev', [(d, d ^ owned_mask(d, lo...  9.17 us
  transfers between devices with their start and end apart: 6, of which 5 were waited for; matrix products, arithmetic and copies ran while one was open for 2% of the time, Pallas kernels for 8%

profile of v3, /device:TPU:0, one launch (start us, length us, event | category | flops | bytes accessed | tf_op | source)
XLA Modules:
  0.0 258.1 jit_solution(637935206670120356)
XLA Ops:
  0.0 13.2 %condition_and_place_0.1 = bf16[32,4,32,512]{3,2,1,0:T(8,128)(2,1)} custom-call(s32[1]{0:T(128)} %bitcast.9.own_ref, s32[2,32]{1,0:T(2,128)} %partners_ref.3, s32[32,32]{1,0:T(8,128)} %start_ref.3, s32[32,32]{1,0:T(8,128)} %count_ref.3, bf16[1024,4096]{1,0:T(8,128)(2,1)} %rows_ref.3, bf16[8,512,512]{2,1,0:T(8,128)(2,1)} %factor_ref.3), custom_call_target="tpu_custom_call" | custom-call | flops 6442450944 | bytes 10485760 | tf_op jit(solution)/shard_map/condition_and_place_0/pallas_call | solution.py:140
  13.2 7.4 %all-to-all-start.1 = ((bf16[32,4,32,512]{3,2,1,0:T(8,128)(2,1)}), bf16[32,4,32,512]{3,2,1,0:T(8,128)(2,1)}, u32[]{:S(2)}, u32[]{:S(2)}) async-start(bf16[32,4,32,512]{3,2,1,0:T(8,128)(2,1)} %condition_and_place_0.1), calls=%async_computation.1 | async-start | bytes 8388608 | tf_op jit(solution)/shard_map/all_to_all | solution.py:168
  20.7 13.2 %condition_and_place_1.1 = bf16[32,4,32,512]{3,2,1,0:T(8,128)(2,1)} custom-call(s32[1]{0:T(128)} %bitcast.9.own_ref, s32[2,32]{1,0:T(2,128)} %partners_ref.3, s32[32,32]{1,0:T(8,128)} %start_ref.3, s32[32,32]{1,0:T(8,128)} %count_ref.3, bf16[1024,4096]{1,0:T(8,128)(2,1)} %rows_ref.3, bf16[8,512,512]{2,1,0:T(8,128)(2,1)} %factor_ref.3), custom_call_target="tpu_custom_call" | custom-call | flops 6442450944 | bytes 10485760 | tf_op jit(solution)/shard_map/condition_and_place_1/pallas_call | solution.py:140
  33.9 80.6 %all-to-all-done.1.received_ref = bf16[32,4,32,512]{3,2,1,0:T(8,128)(2,1)} async-done(((bf16[32,4,32,512]{3,2,1,0:T(8,128)(2,1)}), bf16[32,4,32,512]{3,2,1,0:T(8,128)(2,1)}, u32[]{:S(2)}, u32[]{:S(2)}) %all-to-all-start.1) | async-done | bytes 4194336 | tf_op jit(solution)/shard_map/all_to_all | solution.py:168
  114.5 4.1 %all-to-all-start = ((bf16[32,4,32,512]{3,2,1,0:T(8,128)(2,1)}), bf16[32,4,32,512]{3,2,1,0:T(8,128)(2,1)}, u32[]{:S(2)}, u32[]{:S(2)}) async-start(bf16[32,4,32,512]{3,2,1,0:T(8,128)(2,1)} %condition_and_place_1.1), calls=%async_computation | async-start | bytes 8388608 | tf_op jit(solution)/shard_map/all_to_all | solution.py:168
  118.6 0.6 fusion.11
  122.0 0.1 fusion
  122.1 0.6 gather_fusion
  122.7 0.1 compare_and_fusion
  122.8 0.2 reduce_window_sum.11
  123.0 0.1 convert_reduce_fusion
  123.2 0.1 select_reduce_fusion
  123.3 0.4 copy.19
  123.7 0.4 copy.18
  124.1 0.7 compare_reduce_fusion
  125.5 1.1 sub.14.arrival_ref
  126.5 0.1 compare_reduce_fusion.1
  126.7 8.2 %compact_and_tiles_0.1.refs_0_ = f32[4,512,512]{2,1,0:T(8,128)} custom-call(s32[1]{0:T(128)} %bitcast.2.edge_ref, s32[4,512,1]{2,1,0:T(8,128)} %sub.14.arrival_ref, bf16[32,4,32,512]{3,2,1,0:T(8,128)(2,1)} %all-to-all-done.1.received_ref), custom_call_target="tpu_custom_call" | custom-call | flops 3221225472 | bytes 8388608 | tf_op jit(solution)/shard_map/compact_and_tiles_0/pallas_call | solution.py:194
  134.9 77.6 %all-to-all-done.received_ref = bf16[32,4,32,512]{3,2,1,0:T(8,128)(2,1)} async-done(((bf16[32,4,32,512]{3,2,1,0:T(8,128)(2,1)}), bf16[32,4,32,512]{3,2,1,0:T(8,128)(2,1)}, u32[]{:S(2)}, u32[]{:S(2)}) %all-to-all-start) | async-done | bytes 4194336 | tf_op jit(solution)/shard_map/all_to_all | solution.py:168
  212.5 7.6 %compact_and_tiles_1.1 = (f32[512,512]{1,0:T(8,128)S(1)}, bf16[512,512]{1,0:T(8,128)(2,1)S(1)}, bf16[512,512]{1,0:T(8,128)(2,1)S(1)}, bf16[512,512]{1,0:T(8,128)(2,1)S(1)}) custom-call(s32[1]{0:T(128)} %bitcast.2.edge_ref, s32[4,512,1]{2,1,0:T(8,128)} %sub.14.arrival_ref, bf16[32,4,32,512]{3,2,1,0:T(8,128)(2,1)} %all-to-all-done.received_ref, ...), custom_call_target="tpu_custom_call" | custom-call | flops 3221225472 | bytes 8388608 | tf_op jit(solution)/shard_map/compact_and_tiles_1/pallas_call | solution.py:194
  220.1 34.8 %conditional.1 = (f32[512,512]{1,0:T(8,128)S(1)}, bf16[512,512]{1,0:T(8,128)(2,1)}) conditional(s32[]{:T(128)} %clamp.3, (bf16[512,512]{1,0:T(8,128)(2,1)S(1)}, f32[512,512]{1,0:T(8,128)S(1)}, bf16[512,512]{1,0:T(8,128)(2,1)S(1)}, bf16[512,512]{1,0:T(8,128)(2,1)S(1)}) %tuple.47, (bf16[512,512]{1,0:T(8,128)(2,1)S(1)}, ...), branch_computations={%region_4.5_spmd, %region_5.6_spmd, %region_6.7_spmd, %region_7.8_... | conditional | flops 1835008 | bytes 12583088 | solution.py:224
  220.1 0.6 collective-permute-start
  220.7 0.9 collective-permute-start.1
  221.6 0.8 collective-permute-start.2
  222.3 12.1 %collective-permute-done = bf16[512,512]{1,0:T(8,128)(2,1)S(1)} collective-permute-done((bf16[512,512]{1,0:T(8,128)(2,1)S(1)}, bf16[512,512]{1,0:T(8,128)(2,1)S(1)}, u32[]{:S(2)}, u32[]{:S(2)}) %collective-permute-start) | collective-permute-done | bytes 524320 | tf_op jit(solution)/shard_map/cond/branch_0_fun/ppermute | solution.py:112
  234.4 10.9 %collective-permute-done.2 = bf16[512,512]{1,0:T(8,128)(2,1)S(1)} collective-permute-done((bf16[512,512]{1,0:T(8,128)(2,1)S(1)}, bf16[512,512]{1,0:T(8,128)(2,1)S(1)}, u32[]{:S(2)}, u32[]{:S(2)}) %collective-permute-start.2) | collective-permute-done | bytes 524320 | tf_op jit(solution)/shard_map/cond/branch_0_fun/ppermute | solution.py:112
  245.3 0.3 fusion.1
  245.6 0.1 collective-permute-start.3
  245.7 9.2 %collective-permute-done.3 = bf16[512,512]{1,0:T(8,128)(2,1)} collective-permute-done((bf16[512,512]{1,0:T(8,128)(2,1)S(1)}, bf16[512,512]{1,0:T(8,128)(2,1)}, u32[]{:S(2)}, u32[]{:S(2)}) %collective-permute-start.3) | collective-permute-done | bytes 524320 | tf_op jit(solution)/shard_map/cond/branch_0_fun/ppermute | solution.py:114
  254.9 1.2 convert_bitcast_fusion
  256.1 0.3 copy.20
  256.4 1.7 broadcast_select_fusion
  (13 shorter events, 0.3 us)
Async XLA Ops:
  13.2 101.3 %all-to-all-start.1 = ((bf16[32,4,32,512]{3,2,1,0:T(8,128)(2,1)}), bf16[32,4,32,512]{3,2,1,0:T(8,128)(2,1)}, u32[]{:S(2)}, u32[]{:S(2)}) async-start(bf16[32,4,32,512]{3,2,1,0:T(8,128)(2,1)} %condition_and_place_0.1), calls=%async_computation.1 | async-start | bytes 8388608 | tf_op jit(solution)/shard_map/all_to_all | solution.py:168
  33.9 84.7 %copy-start.1 = (s32[2,32]{1,0:T(2,128)S(1)}, s32[2,32]{1,0:T(2,128)}, u32[]{:S(2)}) copy-start(s32[2,32]{1,0:T(2,128)} %partners_ref.3) | copy-start | bytes 772
  33.9 88.0 %copy-start = (s32[32,32]{1,0:T(8,128)S(1)}, s32[32,32]{1,0:T(8,128)}, u32[]{:S(2)}) copy-start(s32[32,32]{1,0:T(8,128)} %count_ref.3) | copy-start | bytes 12292
  33.9 90.2 %copy-start.2 = (s32[10]{0:T(128)S(1)}, s32[10]{0:T(128)}, u32[]{:S(2)}) copy-start(s32[10]{0:T(128)} %constant.44.clone) | copy-start | bytes 124
  114.5 98.0 %all-to-all-start = ((bf16[32,4,32,512]{3,2,1,0:T(8,128)(2,1)}), bf16[32,4,32,512]{3,2,1,0:T(8,128)(2,1)}, u32[]{:S(2)}, u32[]{:S(2)}) async-start(bf16[32,4,32,512]{3,2,1,0:T(8,128)(2,1)} %condition_and_place_1.1), calls=%async_computation | async-start | bytes 8388608 | tf_op jit(solution)/shard_map/all_to_all | solution.py:168
  220.1 14.3 %collective-permute-start = (bf16[512,512]{1,0:T(8,128)(2,1)S(1)}, bf16[512,512]{1,0:T(8,128)(2,1)S(1)}, u32[]{:S(2)}, u32[]{:S(2)}) collective-permute-start(bf16[512,512]{1,0:T(8,128)(2,1)S(1)} %get-tuple-element.86), channel_id=1, source_target_pairs={{0,3},{1,2},{2,1},{3,0},{4,7},{5,6},{6,5},{7,4},{8,11},{9,10},{10,... | collective-permute-start | bytes 1572872 | tf_op jit(solution)/shard_map/cond/branch_0_fun/ppermute | solution.py:112
  220.7 13.7 %collective-permute-start.1 = (bf16[512,512]{1,0:T(8,128)(2,1)S(1)}, bf16[512,512]{1,0:T(8,128)(2,1)S(1)}, u32[]{:S(2)}, u32[]{:S(2)}) collective-permute-start(bf16[512,512]{1,0:T(8,128)(2,1)S(1)} %get-tuple-element.87), channel_id=1, source_target_pairs={{0,1},{1,0},{2,3},{3,2},{4,5},{5,4},{6,7},{7,6},{8,9},{9,8},{10,11... | collective-permute-start | bytes 1572872 | tf_op jit(solution)/shard_map/cond/branch_0_fun/ppermute | solution.py:112
  221.6 23.7 %collective-permute-start.2 = (bf16[512,512]{1,0:T(8,128)(2,1)S(1)}, bf16[512,512]{1,0:T(8,128)(2,1)S(1)}, u32[]{:S(2)}, u32[]{:S(2)}) collective-permute-start(bf16[512,512]{1,0:T(8,128)(2,1)S(1)} %get-tuple-element.88), channel_id=1, source_target_pairs={{0,2},{1,3},{2,0},{3,1},{4,6},{5,7},{6,4},{7,5},{8,10},{9,11},{10,... | collective-permute-start | bytes 1572872 | tf_op jit(solution)/shard_map/cond/branch_0_fun/ppermute | solution.py:112
  245.6 9.3 %collective-permute-start.3 = (bf16[512,512]{1,0:T(8,128)(2,1)S(1)}, bf16[512,512]{1,0:T(8,128)(2,1)}, u32[]{:S(2)}, u32[]{:S(2)}) collective-permute-start(bf16[512,512]{1,0:T(8,128)(2,1)S(1)} %get-tuple-element.139), channel_id=1, source_target_pairs={{0,1},{1,3},{2,0},{3,2},{4,5},{5,7},{6,4},{7,6},{8,9},{9,11},{10,8... | collective-permute-start | bytes 1572872 | tf_op jit(solution)/shard_map/cond/branch_0_fun/ppermute | solution.py:114

commit v4 on v3

--- a/solution.py
+++ b/solution.py
@@ -107,10 +107,17 @@
 
 def exchange(low, high, own, s1, s2, s3):
     devices = lax.axis_size("dev")
-    total = own
-    for value, mask in ((s3, low ^ high), (s1, low), (s2, high)):
+
+    def across(value, mask):
         got = lax.ppermute(value, "dev", [(d, d ^ mask) for d in range(devices)])
-        total = total + got.astype(jnp.float32)
+        return got.astype(jnp.float32)
+
+    if low == 1:
+        pair = s2.astype(jnp.float32) + across(s3, low)
+        total = own + across(s1, low)
+        total = total + across(pair.astype(jnp.bfloat16), high)
+    else:
+        total = own + across(s3, low ^ high) + across(s1, low) + across(s2, high)
     other = lax.ppermute(
         total.astype(jnp.bfloat16),
         "dev",

time: 261 us -> 250 us (0.958)
  waiting for transfers between devices: 190 us -> 182 us
    ppermute x3, waiting for transfers between devices: 23 us -> 14.1 us  [across(): got = lax.ppermute(value, 'dev', [(d, d ^ mask) for d in range(devices)])]
  transfers between devices with their start and end apart: 6 -> 6, of which waited for: 5 -> 5; matrix products, arithmetic and copies ran while one was open for 2% -> 2% of each run, Pallas kernels for 8% -> 9%
where the time goes in v4:
time: 250 us; the launch traced here: 249 us
  waiting for transfers between devices  182 us (73%)
  Pallas kernels  42.3 us (17%)
  starting transfers between devices  13.4 us (5%)
  other arithmetic  5.97 us (2%)
  between operations  3.21 us (1%)
    all_to_all x2, waiting for transfers between devices, per_device(): lax.all_to_all(send, 'dev', split_axis=0, concat_axis=0, tiled=True)  159 us
    pallas_call x2, Pallas kernels, per_device(): pl.pallas_call(scatter_kernel, out_shape=jax.ShapeDtypeStruct((devices, 4...  26.4 us
    pallas_call x2, Pallas kernels, per_device(): pl.pallas_call(partial(tiles_kernel, scaling=feat_width ** (-0.5), first=...  15.8 us
    ppermute x3, waiting for transfers between devices, across(): got = lax.ppermute(value, 'dev', [(d, d ^ mask) for d in range(devices)])  14.1 us
    all_to_all x2, starting transfers between devices, per_device(): lax.all_to_all(send, 'dev', split_axis=0, concat_axis=0, tiled=True)  11.5 us
    ppermute x1, waiting for transfers between devices, exchange(): lax.ppermute(total.astype(jnp.bfloat16), 'dev', [(d, d ^ owned_mask(d, lo...  9.27 us
  transfers between devices with their start and end apart: 6, of which 5 were waited for; matrix products, arithmetic and copies ran while one was open for 2% of the time, Pallas kernels for 9%

profile of v4, /device:TPU:0, one launch (start us, length us, event | category | flops | bytes accessed | tf_op | source)
XLA Modules:
  0.0 249.1 jit_solution(13208579056901716175)
XLA Ops:
  0.0 13.2 %condition_and_place_0.1 = bf16[32,4,32,512]{3,2,1,0:T(8,128)(2,1)} custom-call(s32[1]{0:T(128)} %bitcast.9.own_ref, s32[2,32]{1,0:T(2,128)} %partners_ref.3, s32[32,32]{1,0:T(8,128)} %start_ref.3, s32[32,32]{1,0:T(8,128)} %count_ref.3, bf16[1024,4096]{1,0:T(8,128)(2,1)} %rows_ref.3, bf16[8,512,512]{2,1,0:T(8,128)(2,1)} %factor_ref.3), custom_call_target="tpu_custom_call" | custom-call | flops 6442450944 | bytes 10485760 | tf_op jit(solution)/shard_map/condition_and_place_0/pallas_call | solution.py:147
  13.2 7.4 %all-to-all-start.1 = ((bf16[32,4,32,512]{3,2,1,0:T(8,128)(2,1)}), bf16[32,4,32,512]{3,2,1,0:T(8,128)(2,1)}, u32[]{:S(2)}, u32[]{:S(2)}) async-start(bf16[32,4,32,512]{3,2,1,0:T(8,128)(2,1)} %condition_and_place_0.1), calls=%async_computation.1 | async-start | bytes 8388608 | tf_op jit(solution)/shard_map/all_to_all | solution.py:175
  20.7 13.2 %condition_and_place_1.1 = bf16[32,4,32,512]{3,2,1,0:T(8,128)(2,1)} custom-call(s32[1]{0:T(128)} %bitcast.9.own_ref, s32[2,32]{1,0:T(2,128)} %partners_ref.3, s32[32,32]{1,0:T(8,128)} %start_ref.3, s32[32,32]{1,0:T(8,128)} %count_ref.3, bf16[1024,4096]{1,0:T(8,128)(2,1)} %rows_ref.3, bf16[8,512,512]{2,1,0:T(8,128)(2,1)} %factor_ref.3), custom_call_target="tpu_custom_call" | custom-call | flops 6442450944 | bytes 10485760 | tf_op jit(solution)/shard_map/condition_and_place_1/pallas_call | solution.py:147
  33.9 80.6 %all-to-all-done.1.received_ref = bf16[32,4,32,512]{3,2,1,0:T(8,128)(2,1)} async-done(((bf16[32,4,32,512]{3,2,1,0:T(8,128)(2,1)}), bf16[32,4,32,512]{3,2,1,0:T(8,128)(2,1)}, u32[]{:S(2)}, u32[]{:S(2)}) %all-to-all-start.1) | async-done | bytes 4194336 | tf_op jit(solution)/shard_map/all_to_all | solution.py:175
  114.5 4.1 %all-to-all-start = ((bf16[32,4,32,512]{3,2,1,0:T(8,128)(2,1)}), bf16[32,4,32,512]{3,2,1,0:T(8,128)(2,1)}, u32[]{:S(2)}, u32[]{:S(2)}) async-start(bf16[32,4,32,512]{3,2,1,0:T(8,128)(2,1)} %condition_and_place_1.1), calls=%async_computation | async-start | bytes 8388608 | tf_op jit(solution)/shard_map/all_to_all | solution.py:175
  118.7 0.5 fusion.11
  121.7 0.1 fusion
  121.8 0.6 gather_fusion
  122.4 0.1 compare_and_fusion
  122.5 0.1 broadcast_select_fusion.1
  122.5 0.2 reduce_window_sum.11
  122.8 0.1 convert_reduce_fusion
  122.9 0.1 select_reduce_fusion
  123.1 0.4 copy.19
  123.5 0.4 copy.18
  123.9 0.7 compare_reduce_fusion
  125.2 1.1 sub.14.arrival_ref
  126.3 0.1 compare_reduce_fusion.1
  126.4 8.2 %compact_and_tiles_0.1.refs_0_ = f32[4,512,512]{2,1,0:T(8,128)} custom-call(s32[1]{0:T(128)} %bitcast.2.edge_ref, s32[4,512,1]{2,1,0:T(8,128)} %sub.14.arrival_ref, bf16[32,4,32,512]{3,2,1,0:T(8,128)(2,1)} %all-to-all-done.1.received_ref), custom_call_target="tpu_custom_call" | custom-call | flops 3221225472 | bytes 8388608 | tf_op jit(solution)/shard_map/compact_and_tiles_0/pallas_call | solution.py:201
  134.6 77.9 %all-to-all-done.received_ref = bf16[32,4,32,512]{3,2,1,0:T(8,128)(2,1)} async-done(((bf16[32,4,32,512]{3,2,1,0:T(8,128)(2,1)}), bf16[32,4,32,512]{3,2,1,0:T(8,128)(2,1)}, u32[]{:S(2)}, u32[]{:S(2)}) %all-to-all-start) | async-done | bytes 4194336 | tf_op jit(solution)/shard_map/all_to_all | solution.py:175
  212.5 7.6 %compact_and_tiles_1.1 = (f32[512,512]{1,0:T(8,128)S(1)}, bf16[512,512]{1,0:T(8,128)(2,1)S(1)}, bf16[512,512]{1,0:T(8,128)(2,1)S(1)}, bf16[512,512]{1,0:T(8,128)(2,1)S(1)}) custom-call(s32[1]{0:T(128)} %bitcast.2.edge_ref, s32[4,512,1]{2,1,0:T(8,128)} %sub.14.arrival_ref, bf16[32,4,32,512]{3,2,1,0:T(8,128)(2,1)} %all-to-all-done.received_ref, ...), custom_call_target="tpu_custom_call" | custom-call | flops 3221225472 | bytes 8388608 | tf_op jit(solution)/shard_map/compact_and_tiles_1/pallas_call | solution.py:201
  220.1 25.7 %conditional.1 = (f32[512,512]{1,0:T(8,128)S(1)}, bf16[512,512]{1,0:T(8,128)(2,1)}) conditional(s32[]{:T(128)} %clamp.3, (bf16[512,512]{1,0:T(8,128)(2,1)S(1)}, f32[512,512]{1,0:T(8,128)S(1)}, bf16[512,512]{1,0:T(8,128)(2,1)S(1)}, bf16[512,512]{1,0:T(8,128)(2,1)S(1)}) %tuple.47, (bf16[512,512]{1,0:T(8,128)(2,1)S(1)}, ...), branch_computations={%region_4.5_spmd, %region_5.6_spmd, %region_6.7_spmd, %region_7.8_... | conditional | flops 2359296 | bytes 13631664 | solution.py:231
  220.2 0.5 collective-permute-start
  220.7 1.4 collective-permute-done.1
  222.1 0.1 add_convert_fusion
  222.3 1.3 collective-permute-start.2
  223.6 12.7 %collective-permute-done.2 = bf16[512,512]{1,0:T(8,128)(2,1)S(1)} collective-permute-done((bf16[512,512]{1,0:T(8,128)(2,1)S(1)}, bf16[512,512]{1,0:T(8,128)(2,1)S(1)}, u32[]{:S(2)}, u32[]{:S(2)}) %collective-permute-start.2) | collective-permute-done | bytes 524320 | tf_op jit(solution)/shard_map/cond/branch_0_fun/ppermute | solution.py:112
  236.3 0.2 fusion.1
  236.6 9.3 %collective-permute-done.3 = bf16[512,512]{1,0:T(8,128)(2,1)} collective-permute-done((bf16[512,512]{1,0:T(8,128)(2,1)S(1)}, bf16[512,512]{1,0:T(8,128)(2,1)}, u32[]{:S(2)}, u32[]{:S(2)}) %collective-permute-start.3) | collective-permute-done | bytes 524320 | tf_op jit(solution)/shard_map/cond/branch_0_fun/ppermute | solution.py:121
  245.8 1.2 convert_bitcast_fusion
  247.0 0.3 copy.20
  247.4 1.7 broadcast_select_fusion
  (14 shorter events, 0.3 us)
Async XLA Ops:
  13.2 101.3 %all-to-all-start.1 = ((bf16[32,4,32,512]{3,2,1,0:T(8,128)(2,1)}), bf16[32,4,32,512]{3,2,1,0:T(8,128)(2,1)}, u32[]{:S(2)}, u32[]{:S(2)}) async-start(bf16[32,4,32,512]{3,2,1,0:T(8,128)(2,1)} %condition_and_place_0.1), calls=%async_computation.1 | async-start | bytes 8388608 | tf_op jit(solution)/shard_map/all_to_all | solution.py:175
  33.9 84.8 %copy-start.1 = (s32[2,32]{1,0:T(2,128)S(1)}, s32[2,32]{1,0:T(2,128)}, u32[]{:S(2)}) copy-start(s32[2,32]{1,0:T(2,128)} %partners_ref.3) | copy-start | bytes 772
  33.9 87.7 %copy-start = (s32[32,32]{1,0:T(8,128)S(1)}, s32[32,32]{1,0:T(8,128)}, u32[]{:S(2)}) copy-start(s32[32,32]{1,0:T(8,128)} %count_ref.3) | copy-start | bytes 12292
  33.9 89.9 %copy-start.2 = (s32[10]{0:T(128)S(1)}, s32[10]{0:T(128)}, u32[]{:S(2)}) copy-start(s32[10]{0:T(128)} %constant.44.clone) | copy-start | bytes 124
  114.5 98.0 %all-to-all-start = ((bf16[32,4,32,512]{3,2,1,0:T(8,128)(2,1)}), bf16[32,4,32,512]{3,2,1,0:T(8,128)(2,1)}, u32[]{:S(2)}, u32[]{:S(2)}) async-start(bf16[32,4,32,512]{3,2,1,0:T(8,128)(2,1)} %condition_and_place_1.1), calls=%async_computation | async-start | bytes 8388608 | tf_op jit(solution)/shard_map/all_to_all | solution.py:175
  220.2 2.0 collective-permute-start.1
  220.2 3.4 %collective-permute-start = (bf16[512,512]{1,0:T(8,128)(2,1)S(1)}, bf16[512,512]{1,0:T(8,128)(2,1)S(1)}, u32[]{:S(2)}, u32[]{:S(2)}) collective-permute-start(bf16[512,512]{1,0:T(8,128)(2,1)S(1)} %get-tuple-element.86), channel_id=1, source_target_pairs={{0,1},{1,0},{2,3},{3,2},{4,5},{5,4},{6,7},{7,6},{8,9},{9,8},{10,11... | collective-permute-start | bytes 1572872 | tf_op jit(solution)/shard_map/cond/branch_0_fun/ppermute | solution.py:112
  222.3 14.0 %collective-permute-start.2 = (bf16[512,512]{1,0:T(8,128)(2,1)S(1)}, bf16[512,512]{1,0:T(8,128)(2,1)S(1)}, u32[]{:S(2)}, u32[]{:S(2)}) collective-permute-start(bf16[512,512]{1,0:T(8,128)(2,1)S(1)} %add_convert_fusion), channel_id=1, source_target_pairs={{0,2},{1,3},{2,0},{3,1},{4,6},{5,7},{6,4},{7,5},{8,10},{9,11},{10,... | collective-permute-start | bytes 1572872 | tf_op jit(solution)/shard_map/cond/branch_0_fun/ppermute | solution.py:112
  236.5 9.3 %collective-permute-start.3 = (bf16[512,512]{1,0:T(8,128)(2,1)S(1)}, bf16[512,512]{1,0:T(8,128)(2,1)}, u32[]{:S(2)}, u32[]{:S(2)}) collective-permute-start(bf16[512,512]{1,0:T(8,128)(2,1)S(1)} %get-tuple-element.139), channel_id=1, source_target_pairs={{0,1},{1,3},{2,0},{3,2},{4,5},{5,7},{6,4},{7,6},{8,9},{9,11},{10,8... | collective-permute-start | bytes 1572872 | tf_op jit(solution)/shard_map/cond/branch_0_fun/ppermute | solution.py:121
